TPU v7x, 128 devices: a whole 4x4x4 slice. The times are simulated.
128 devices in a mesh: dp: 16 (over y, x), tensor: 8 (over z, core).
Axes of the slice: x: 4, y: 4, z: 4, core: 2. Of those that a mesh axis runs over, the one named last changes fastest.
Arguments:
- hidden_input: bfloat16 [16384, 8192], P('dp'), may hold values from -6 to 6
- key_value_gradient: bfloat16 [2, 16384, 1024], P(None, 'dp', 'tensor'), may hold values from -6 to 6
- key_value_weight: bfloat16 [2, 8192, 1024], P(None, None, 'tensor'), may hold values from -0.0625 to 0.0625
- down_adapters: bfloat16 [128, 32, 8192], P(None, None, 'tensor'), may hold values from -0.0625 to 0.0625
- up_adapters: bfloat16 [128, 2, 16, 1024], P(None, None, None, 'tensor'), may hold values from -0.1875 to 0.1875
- adapter_inner_saved: bfloat16 [32, 16384], P(None, 'dp'), may hold values from -2 to 2
- block_owner_tenant: int32 [128], P('dp'), may hold values from 0 to 127
- live_block_counts: int32 [16], P('dp'), may hold values from 1 to 8, as said below
- tenant_position: int32 [128], replicated, may hold values from 0 to 127, each once
Outputs:
- hidden_gradient: bfloat16 [16384, 8192], P('dp', 'tensor')
- grad_a: float32 [128, 32, 8192], P('dp', None, 'tensor')
- grad_b: float32 [128, 2, 16, 1024], P('dp', None, None, 'tensor')
Inputs may be any that keep to these rules, and one draw needn't show every extreme that they name: `live_block_counts`: some index of dp has all 8 block slots live.
All inputs are finite; a program needn't handle non-finite values.
Results may differ from a plain program's by a relative error of at most 0.022.
Values may be sent and summed in bfloat16 or wider, within the bound.
A program may use at most 192 MiB of HBM per device.

v0:
```python
import jax
import jax.numpy as jnp
from jax import lax
from jax.sharding import PartitionSpec as P


def per_device(
    hidden_input,
    key_value_gradient,
    key_value_weight,
    down_adapters,
    up_adapters,
    adapter_inner_saved,
    block_owner_tenant,
    live_block_counts,
    tenant_position,
):
    tok_rows = hidden_input.shape[0]
    block_list = block_owner_tenant.shape[0]
    block_length = tok_rows // block_list
    head_cols = key_value_gradient.shape[2]
    width_cols = down_adapters.shape[2]
    tenants = tenant_position.shape[0]
    rank_row_slice = down_adapters.shape[1]
    live_blk = jnp.arange(block_list, dtype=jnp.int32) < live_block_counts[0]
    live_tok = jnp.broadcast_to(live_blk[:, None], (block_list, block_length)).reshape(tok_rows)
    grad = key_value_gradient * live_tok.astype(jnp.bfloat16)[None, :, None]
    picked = block_owner_tenant[:, None] == jnp.arange(tenants, dtype=jnp.int32)[None, :]
    slot_blk = jnp.sum(jnp.where(picked, tenant_position[None, :], 0), axis=1)
    b_sel = jnp.take(up_adapters, block_owner_tenant, axis=0)
    g_blk = grad.reshape(2, block_list, block_length, head_cols)
    inner_part = jnp.einsum("cbij,bcrj->bicr", g_blk, b_sel, preferred_element_type=jnp.float32)
    inner = lax.psum(inner_part.reshape(tok_rows, rank_row_slice).astype(jnp.bfloat16), "tensor")
    inner_block = inner.reshape(block_list, block_length, rank_row_slice)
    selected_down = jnp.take(down_adapters, block_owner_tenant, axis=0)
    adapter_input_gradient = jnp.einsum(
        "hxr,hrg->hxg", inner_block, selected_down, preferred_element_type=jnp.float32
    ).reshape(tok_rows, width_cols)
    partial_value = jnp.einsum(
        "cnj,cdj->nd", grad, key_value_weight, preferred_element_type=jnp.float32
    )
    base_offset = lax.psum_scatter(
        partial_value.astype(jnp.bfloat16), "tensor", scatter_dimension=1, tiled=True
    ).astype(jnp.float32)
    hidden_gradient = (base_offset + 2.0 * adapter_input_gradient).astype(jnp.bfloat16)
    x_cols = lax.dynamic_slice_in_dim(
        hidden_input, lax.axis_index("tensor") * width_cols, width_cols, 1
    )
    per_a = jnp.einsum(
        "bic,bid->bcd",
        inner_block,
        x_cols.reshape(block_list, block_length, width_cols),
        preferred_element_type=jnp.float32,
    )
    hidden_block = adapter_inner_saved.reshape(2, rank_row_slice // 2, block_list, block_length)
    per_b = jnp.einsum("crbi,cbij->bcrj", hidden_block, g_blk, preferred_element_type=jnp.float32)
    per_block = 2.0 * jnp.concatenate(
        [per_a, per_b.reshape(block_list, rank_row_slice, head_cols)], axis=2
    )
    owned_rows = tenants // lax.axis_size("dp")
    onehot = (
        slot_blk[None, :] == jnp.arange(owned_rows * lax.axis_size("dp"), dtype=jnp.int32)[:, None]
    ).astype(jnp.float32)
    owned = lax.psum_scatter(
        jnp.einsum("sb,bcd->scd", onehot, per_block, precision=lax.Precision.HIGHEST).astype(
            jnp.bfloat16
        ),
        "dp",
        scatter_dimension=0,
        tiled=True,
    ).astype(jnp.float32)
    grad_a = owned[:, :, :width_cols]
    grad_b = owned[:, :, width_cols:].reshape(owned_rows, 2, rank_row_slice // 2, head_cols)
    return (hidden_gradient, grad_a, grad_b)


def solution(mesh):
    return jax.shard_map(
        per_device,
        mesh=mesh,
        in_specs=(
            P("dp", None),
            P(None, "dp", "tensor"),
            P(None, None, "tensor"),
            P(None, None, "tensor"),
            P(None, None, None, "tensor"),
            P(None, "dp"),
            P("dp"),
            P("dp"),
            P(),
        ),
        out_specs=(P("dp", "tensor"), P("dp", None, "tensor"), P("dp", None, None, "tensor")),
        check_vma=False,
    )
```

profile of v0, /device:TPU:1, one launch (start us, length us, event | category | flops | bytes accessed | tf_op | source)
XLA Modules:
  0.0 339.3 jit_solution(14579576244899069147)
XLA Ops:
  7.2 0.0 copy-start
  7.2 0.0 copy-start.5
  7.2 0.0 copy-start.6
  7.2 0.0 all-reduce.4.cloned.1.call-start
  7.2 0.7 compare_select_fusion
  8.0 0.7 compare_and_fusion
  9.3 0.1 broadcast_bitcast_fusion
  9.4 1.2 broadcast_multiply_fusion
  10.6 0.0 copy-done
  10.6 0.0 copy-start.2
  10.7 0.6 gather_fusion
  11.2 1.1 convolution_convert_fusion.1
  12.3 0.0 all-reduce.4.cloned.1.call-update
  12.3 0.0 all-reduce.6.cloned.1.call-start
  12.4 0.9 copy.32
  13.2 0.2 fusion.4
  13.5 0.0 copy-done.2
  13.5 1.8 constant_dynamic-slice_fusion
  15.2 0.0 copy-done.5
  15.2 0.0 copy-done.6
  15.3 0.2 select_reduce_fusion
  15.4 57.1 %all-reduce.4.cloned.1.call-done = bf16[8,128,32]{1,2,0:T(8,128)(2,1)} async-done(((bf16[8,128,32]{1,2,0:T(8,128)(2,1)}), bf16[8,128,32]{1,2,0:T(8,128)(2,1)}) %all-reduce.4.cloned.1.call-update) | async-done | bytes 65552 | tf_op jit(solution)/shard_map/psum | solution.py:33
  72.5 1.2 fusion.17
  73.8 0.1 maximum_multiply_fusion
  73.9 9.9 %convolution_convert_fusion = bf16[128,32,1152]{2,0,1:T(8,128)(2,1)} fusion(f32[8,32,1152]{2,1,0:T(8,128)S(1)} %maximum_multiply_fusion, s32[8]{0:T(128)S(1)} %select_reduce_fusion), kind=kOutput, calls=%fused_computation.3 | convolution fusion | flops 457704448 | bytes 10616864 | tf_op jit(solution)/shard_map/sb,bcd->scd/dot_general | solution.py:65
  83.8 0.0 copy-start.3
  83.8 0.0 all-reduce.6.cloned.1.call-update
  83.8 0.0 reduce-scatter.3.cloned.1.call-start
  83.8 1.0 copy-done.3
  84.8 10.8 %bitcast_convert_fusion = bf16[1024,8192]{1,0:T(8,128)(2,1)} fusion(bf16[2,1024,128]{2,1,0:T(8,128)(2,1)S(1)} %copy-done.3, bf16[2,8192,128]{2,1,0:T(8,128)(2,1)} %param.11), kind=kOutput, calls=%fused_computation.2 | convolution fusion | flops 4303355904 | bytes 21495808 | tf_op jit(solution)/shard_map/cnj,cdj->nd/dot_general | solution.py:39
  95.6 0.0 copy-start.7
  95.6 0.0 copy-start.4
  95.6 0.0 reduce-scatter.3.cloned.1.call-update
  95.6 4.0 %gather_fusion.1 = bf16[8,32,1024]{2,1,0:T(8,128)(2,1)S(1)} fusion(bf16[128,32,1024]{2,1,0:T(8,128)(2,1)} %param.12, s32[1024]{0:T(1024)S(1)} %pad_clamp_fusion), kind=kCustom, calls=%fused_computation.1 | custom fusion | bytes 1048608 | tf_op jit(solution)/shard_map/jit(_take)/gather | solution.py:35
  99.6 0.0 copy-done.7
  99.6 0.6 dynamic-slice
  100.9 0.0 copy-done.4
  100.9 2.7 convolution_multiply_fusion
  103.6 130.9 %all-reduce.6.cloned.1.call-done = bf16[128,32,1152]{2,0,1:T(8,128)(2,1)} async-done(((bf16[128,32,1152]{2,0,1:T(8,128)(2,1)}), bf16[128,32,1152]{2,0,1:T(8,128)(2,1)}) %all-reduce.6.cloned.1.call-update) | async-done | bytes 9437200
  234.5 1.1 dynamic-slice_convert_fusion
  235.6 0.1 slice.12
  235.8 1.6 copy.28
  237.3 0.0 copy-start.1
  237.3 0.7 copy.29
  238.0 89.8 %reduce-scatter.3.cloned.1.call-done = bf16[1024,1024]{1,0:T(8,128)(2,1)} async-done(((bf16[1024,8192]{1,0:T(8,128)(2,1)}), bf16[1024,1024]{1,0:T(8,128)(2,1)}) %reduce-scatter.3.cloned.1.call-update) | async-done | bytes 2097168 | tf_op jit(solution)/shard_map/reduce_scatter | solution.py:42
  327.8 5.0 %fusion = bf16[1024,1024]{1,0:T(8,128)(2,1)} fusion(f32[8,128,1024]{2,1,0:T(8,128)} %convolution_multiply_fusion, bf16[1024,1024]{1,0:T(8,128)(2,1)} %reduce-scatter.3.cloned.1.call-done), kind=kLoop, calls=%fused_computation.5 | loop fusion | flops 3145728 | bytes 8388608 | tf_op jit(solution)/shard_map/convert_element_type | solution.py:45
  332.8 0.0 copy-done.1
  (3 shorter events, 0.0 us)
Async XLA Ops:
  7.2 3.5 %copy-start = (bf16[128,2,16,128]{3,2,1,0:T(8,128)(2,1)S(1)}, bf16[128,2,16,128]{3,2,1,0:T(8,128)(2,1)}, u32[]{:S(2)}) copy-start(bf16[128,2,16,128]{3,2,1,0:T(8,128)(2,1)} %param.13) | copy-start | bytes 3145732
  7.2 8.1 %copy-start.5 = (s32[8]{0:T(128)S(1)}, s32[8]{0:T(128)}, u32[]{:S(2)}) copy-start(s32[8]{0:T(128)} %param.15) | copy-start | bytes 100
  7.2 8.1 %copy-start.6 = (s32[128]{0:T(128)S(1)}, s32[128]{0:T(128)}, u32[]{:S(2)}) copy-start(s32[128]{0:T(128)} %param.17) | copy-start | bytes 1540
  7.2 65.3 %all-reduce.4.cloned.1.call-start = ((), (), s32[]{:S(2)}) async-start(), calls=%async_computation.2 | async-start | bytes 131072 | tf_op jit(solution)/shard_map/psum | solution.py:33
  10.6 2.8 copy-start.2
  12.3 222.2 %all-reduce.6.cloned.1.call-start = ((), (), s32[]{:S(2)}) async-start(), calls=%async_computation.3 | async-start | bytes 18874368
  83.8 1.0 copy-start.3
  83.8 244.0 %reduce-scatter.3.cloned.1.call-start = ((), (), s32[]{:S(2)}) async-start(), calls=%async_computation.1 | async-start | bytes 18874368 | tf_op jit(solution)/shard_map/reduce_scatter | solution.py:42
  95.6 4.0 %copy-start.7 = (u32[128]{0:T(128)S(1)}, u32[128]{0:T(128)}, u32[]{:S(2)}) copy-start(u32[128]{0:T(128)} %constant.44) | copy-start | bytes 1540
  95.6 5.3 %copy-start.4 = (bf16[8,128,32]{1,2,0:T(8,128)(2,1)S(1)}, bf16[8,128,32]{1,2,0:T(8,128)(2,1)}, u32[]{:S(2)}) copy-start(bf16[8,128,32]{1,2,0:T(8,128)(2,1)} %all-reduce.4.cloned.1.call-done) | copy-start | bytes 196612
  237.3 95.4 %copy-start.1 = (bf16[128,2,16,128]{3,2,1,0:T(8,128)(2,1)S(1)}, bf16[128,2,16,128]{3,2,1,0:T(8,128)(2,1)}, u32[]{:S(2)}) copy-start(bf16[128,2,16,128]{3,2,1,0:T(8,128)(2,1)} %param.13) | copy-start | bytes 3145732
Sparse Core Ops, SparseCore 0:
  12.4 60.0 all-reduce.3
  83.9 150.5 all-reduce.5
  236.9 90.8 reduce-scatter.2
where the time goes:
time: 340 us; the launch traced here: 339 us
  waiting for transfers between devices  278 us (82%)
  matrix products  25.9 us (8%)
  between operations  15.2 us (4%)
  local copies, waits for them, and re-layouts  11.2 us (3%)
  other arithmetic  9.03 us (3%)
    unnamed x4, waiting for transfers between devices  131 us
    reduce_scatter x1, waiting for transfers between devices, per_device(): lax.psum_scatter(partial_value.astype(jnp.bfloat16), 'tensor', scatter_di...  89.8 us
    psum x1, waiting for transfers between devices, per_device(): lax.psum(inner_part.reshape(tok_rows, rank_row_slice).astype(jnp.bfloat16...  57.1 us
    dot_general x1, matrix products, per_device(): jnp.einsum('cnj,cdj->nd', grad, key_value_weight, preferred_element_type=...  10.8 us
    dot_general x1, matrix products, per_device(): jnp.einsum('sb,bcd->scd', onehot, per_block, precision=lax.Precision.HIGH...  9.89 us
  transfers between devices with their start and end apart: 3, of which 3 were waited for; matrix products, arithmetic and copies ran while one was open for 7% of the time, Pallas kernels for 0%

commit v1 on v0

v1 whole, which is shorter than its diff:
```python
import jax
import jax.numpy as jnp
from jax import lax
from jax.experimental import pallas as pl
from jax.experimental.pallas import tpu as pltpu
from jax.sharding import PartitionSpec as P

MESH = pl.DeviceIdType.MESH
BF = jnp.bfloat16
F32 = jnp.float32
NT = (((1,), (1,)), ((), ()))
N_REMOTE = 80
N_LOCAL = 12


def comm_kernel(
    x_hbm, kvg_hbm, w_hbm, down_hbm, up_hbm, inner_hbm, owner_ref, live_ref, tp_ref,
    hg_hbm, ga_hbm, gb_hbm,
    gf, wf, xv, downv, upv, innerv, kvgv,
    upart, urecv, uz, ubf, ubd, asel,
    meta_a, meta_b, ea, eb, aga, agb,
    snd_a, snd_b, r1_a, r1_b, r2_a, r2_b, own_a, own_b, dns_a, dns_b,
    hgv, gav, gbv,
    ss, rs, ls,
):
    dp = lax.axis_index("dp")
    t = lax.axis_index("tensor")
    y, x = dp // 4, dp % 4
    z, c = t // 2, t % 2

    def xdev(d):
        return (y * 4 + (x + d) % 4, t)

    def ydev(d):
        return (((y + d) % 4) * 4 + x, t)

    def zdev(d, rel):
        return (dp, ((z + d) % 4) * 2 + (c + rel) % 2)

    sib = zdev(0, 1)
    count = [0, 0]
    pending = []

    def rcopy(src, dst, dev):
        k = count[0]
        count[0] += 1
        cp = pltpu.make_async_remote_copy(
            src_ref=src, dst_ref=dst, send_sem=ss.at[k], recv_sem=rs.at[k],
            device_id=dev, device_id_type=MESH,
        )
        cp.start()
        pending.append(cp)
        return cp

    def lcopy(src, dst):
        k = count[1]
        count[1] += 1
        cp = pltpu.make_async_copy(src, dst, ls.at[k])
        cp.start()
        return cp

    peers = [sib]
    peers += [zdev(d, rel) for d in (1, 2, 3) for rel in (0, 1)]
    peers += [xdev(d) for d in (1, 2, 3)] + [ydev(d) for d in (1, 2, 3)]
    barrier = pltpu.get_barrier_semaphore()
    for dev in peers:
        pl.semaphore_signal(barrier, inc=1, device_id=dev, device_id_type=MESH)

    l_kvg = lcopy(kvg_hbm, kvgv)
    l_up = lcopy(up_hbm, upv)
    l_inner = lcopy(inner_hbm, innerv)
    l_w = lcopy(w_hbm.at[:, pl.ds(t * 1024, 1024), :], wf.at[0])
    l_x = lcopy(x_hbm.at[:, pl.ds(t * 1024, 1024)], xv)
    l_down = lcopy(down_hbm, downv)

    lane = lax.broadcasted_iota(jnp.int32, (8, 128), 1)
    pos = jnp.zeros((8, 128), jnp.int32)
    for b in range(8):
        pos = jnp.where((lane >> 4) == b, tp_ref[owner_ref[b]], pos)
    meta_a[0] = pos
    meta_b[0] = pos

    pl.semaphore_wait(barrier, len(peers))

    qa = y * 4 + x
    qb = x * 4 + y
    w1 = []
    for d in (1, 2, 3):
        for rel in (0, 1):
            slot = (4 - d) * 2 + rel
            q = qa if slot < 5 else qb
            dst_t = ((z + d) % 4) * 2 + (c + rel) % 2
            w1.append(
                rcopy(
                    w_hbm.at[:, pl.ds(dst_t * 1024 + q * 64, 64), :],
                    wf.at[slot, :, pl.ds(q * 64, 64), :],
                    zdev(d, rel),
                )
            )
    m1 = []
    for d in (1, 2, 3):
        m1.append(rcopy(meta_a.at[0], meta_a.at[4 - d], xdev(d)))
        m1.append(rcopy(meta_b.at[0], meta_b.at[4 - d], ydev(d)))

    l_kvg.wait()
    l_up.wait()
    live = live_ref[0]
    for b in range(8):
        rows = pl.ds(b * 128, 128)
        upb = upv[owner_ref[b]]
        for ch in range(2):
            g = kvgv[ch, rows, :]
            g = jnp.where(b < live, g, jnp.zeros_like(g))
            gf[0, ch, rows, :] = g
            upart[b // 4, ch * 16:(ch + 1) * 16, (b % 4) * 128:(b % 4 + 1) * 128] = (
                lax.dot_general(upb[ch * 16:(ch + 1) * 16], g, NT, preferred_element_type=F32)
            )
    u1 = rcopy(upart.at[1 - c], urecv, sib)
    l_inner.wait()
    for b in range(8):
        rows = pl.ds(b * 128, 128)
        for ch, ag in ((0, aga), (1, agb)):
            ag[b * 16:(b + 1) * 16, 1024:1152] = jnp.dot(
                innerv[ch * 16:(ch + 1) * 16, b * 128:(b + 1) * 128], gf[0, ch, rows, :],
                preferred_element_type=F32,
            ).astype(BF)
    u1.wait_recv()
    uz[0] = (upart[c] + urecv[...]).astype(BF)
    u2 = [rcopy(uz.at[0], uz.at[4 - d], zdev(d, 0)) for d in (1, 3, 2)]
    g_r = rcopy(gf.at[0], gf.at[6], zdev(1, 0))
    g_l = rcopy(gf.at[0], gf.at[2], zdev(3, 0))
    g_s = [rcopy(gf.at[0], gf.at[1], sib)]

    for cp in w1:
        cp.wait_recv()
    half_a, half_b = pl.ds(2, 3), pl.ds(5, 3)

    def wslice(half, row, size):
        return wf.at[half, :, pl.ds(row, size), :]

    def own_send(half, row, size, dev):
        return rcopy(wslice(half, row, size), wslice(half, row, size), dev)

    wa_r = own_send(half_a, qa * 64, 64, xdev(1))
    wa_l = own_send(half_a, qa * 64, 64, xdev(3))
    wb_r = own_send(half_b, qb * 64, 64, ydev(1))
    wb_l = own_send(half_b, qb * 64, 64, ydev(3))
    w_s = rcopy(w_hbm.at[:, pl.ds(sib[1] * 1024, 1024), :], wf.at[1], sib)

    for cp in u2:
        cp.wait_recv()
    ubf[c] = (
        uz[0].astype(F32) + uz[1].astype(F32) + uz[2].astype(F32) + uz[3].astype(F32)
    ).astype(BF)
    u3 = rcopy(ubf.at[c], ubf.at[c], sib)

    xl, xr = (x + 3) % 4, (x + 1) % 4
    yd, yu = (y + 3) % 4, (y + 1) % 4
    wa_r.wait_recv()
    wa_l.wait_recv()
    wa_o1 = own_send(half_a, (y * 4 + xl) * 64, 32, xdev(1))
    wa_o2 = own_send(half_a, (y * 4 + xr) * 64 + 32, 32, xdev(3))
    wb_r.wait_recv()
    wb_l.wait_recv()
    wb_o1 = own_send(half_b, (x * 4 + yd) * 64, 32, ydev(1))
    wb_o2 = own_send(half_b, (x * 4 + yu) * 64 + 32, 32, ydev(3))

    u3.wait_recv()
    l_x.wait()
    for b in range(8):
        ub = ubf[b // 4, :, (b % 4) * 128:(b % 4 + 1) * 128]
        term = jnp.dot(ub, xv[b * 128:(b + 1) * 128, :], preferred_element_type=F32).astype(BF)
        aga[b * 16:(b + 1) * 16, 0:1024] = term[0:16]
        agb[b * 16:(b + 1) * 16, 0:1024] = term[16:32]

    def row(ref, start, size):
        return ref.at[pl.ds(start, size), :]

    a_r = rcopy(row(aga, 0, 128), row(aga, 384, 128), xdev(1))
    a_l = rcopy(row(aga, 0, 128), row(aga, 128, 128), xdev(3))
    b_r = rcopy(row(agb, 0, 128), row(agb, 384, 128), ydev(1))
    b_l = rcopy(row(agb, 0, 128), row(agb, 128, 128), ydev(3))

    wa_o1.wait_recv()
    wa_o2.wait_recv()
    wa2_r = own_send(half_a, y * 256, 256, ydev(1))
    wa2_l = own_send(half_a, y * 256, 256, ydev(3))
    wb_o1.wait_recv()
    wb_o2.wait_recv()
    wb2_r = own_send(half_b, x * 256, 256, xdev(1))
    wb2_l = own_send(half_b, x * 256, 256, xdev(3))

    for cp in m1:
        cp.wait_recv()
    out_row = lax.broadcasted_iota(jnp.int32, (512, 128), 0)
    lane1 = lax.broadcasted_iota(jnp.int32, (1, 128), 1)
    for s in range(4):
        for meta, e, ring, other, mine in (
            (meta_a, ea, 0, 2, (x, y)), (meta_b, eb, 2, 0, (y, x)),
        ):
            p = meta[s, 0:1, :]
            owner = p >> 3
            valid = ((owner >> ring) & 3) == mine[0]
            dest = (((owner >> other) & 3) - mine[1]) & 3
            target = jnp.where(valid, dest * 128 + (p & 7) * 16 + (lane1 & 15), -1)
            e[:, s * 128:(s + 1) * 128] = (out_row == target).astype(F32).astype(BF)

    l_down.wait()
    for b in range(8):
        asel[b * 32:(b + 1) * 32, :] = downv[owner_ref[b]]
        ub = 2.0 * ubf[b // 4, :, (b % 4) * 128:(b % 4 + 1) * 128].astype(F32)
        parts = []
        if b > 0:
            parts.append(jnp.zeros((b * 32, 128), F32))
        parts.append(ub)
        if b < 7:
            parts.append(jnp.zeros(((7 - b) * 32, 128), F32))
        ubd[b * 128:(b + 1) * 128, :] = jnp.concatenate(parts, axis=0).T.astype(BF)

    a_r.wait_recv()
    a_l.wait_recv()
    a_o1 = rcopy(row(aga, 384, 64), row(aga, 256, 64), xdev(1))
    a_o2 = rcopy(row(aga, 192, 64), row(aga, 320, 64), xdev(3))
    b_r.wait_recv()
    b_l.wait_recv()
    b_o1 = rcopy(row(agb, 384, 64), row(agb, 256, 64), ydev(1))
    b_o2 = rcopy(row(agb, 192, 64), row(agb, 320, 64), ydev(3))

    first, last = pl.ds(0, 512), pl.ds(512, 512)
    g_r.wait_recv()
    g_l.wait_recv()
    g_o1 = rcopy(gf.at[6, :, first, :], gf.at[4, :, first, :], zdev(1, 0))
    g_o2 = rcopy(gf.at[2, :, last, :], gf.at[4, :, last, :], zdev(3, 0))
    g_s.append(rcopy(gf.at[6], gf.at[7], sib))
    g_s.append(rcopy(gf.at[2], gf.at[3], sib))

    wa2_r.wait_recv()
    wa2_l.wait_recv()
    wa2_o1 = own_send(half_a, yd * 256, 128, ydev(1))
    wa2_o2 = own_send(half_a, yu * 256 + 128, 128, ydev(3))
    wb2_r.wait_recv()
    wb2_l.wait_recv()
    wb2_o1 = own_send(half_b, xl * 256, 128, xdev(1))
    wb2_o2 = own_send(half_b, xr * 256 + 128, 128, xdev(3))

    def gathered(e, ag, k):
        return jnp.dot(e[k * 128:(k + 1) * 128, :], ag[...], preferred_element_type=F32)

    rings = ((a_o1, a_o2, ea, aga, snd_a, r1_a, r2_a, own_a, dns_a, ydev),
             (b_o1, b_o2, eb, agb, snd_b, r1_b, r2_b, own_b, dns_b, xdev))
    steps = []
    for o1, o2, e, ag, snd, r1, r2, own, dns, dev in rings:
        o1.wait_recv()
        o2.wait_recv()
        snd[256:384, :] = gathered(e, ag, 2).astype(BF)
        s1 = rcopy(row(snd, 256, 64), row(r1, 0, 64), dev(1))
        s2 = rcopy(row(snd, 320, 64), row(r1, 64, 64), dev(3))
        up = gathered(e, ag, 1)
        snd[192:256, :] = up[64:128].astype(BF)
        dns[0:64, :] = up[0:64]
        s3 = rcopy(row(snd, 192, 64), row(r2, 64, 64), dev(1))
        dn = gathered(e, ag, 3)
        snd[384:448, :] = dn[0:64].astype(BF)
        dns[64:128, :] = dn[64:128]
        s4 = rcopy(row(snd, 384, 64), row(r2, 128, 64), dev(3))
        own[...] = gathered(e, ag, 0)
        steps.append((s1, s2, s3, s4))
    g_o1.wait_recv()
    g_o2.wait_recv()
    g_s.append(rcopy(gf.at[4], gf.at[5], sib))
    lasts = []
    for (s1, s2, s3, s4), (o1, o2, e, ag, snd, r1, r2, own, dns, dev) in zip(steps, rings):
        s1.wait_recv()
        snd[128:192, :] = (dns[0:64, :] + r1[0:64, :].astype(F32)).astype(BF)
        s5 = rcopy(row(snd, 128, 64), row(r2, 0, 64), dev(1))
        s2.wait_recv()
        snd[448:512, :] = (dns[64:128, :] + r1[64:128, :].astype(F32)).astype(BF)
        s6 = rcopy(row(snd, 448, 64), row(r2, 192, 64), dev(3))
        lasts.append((s3, s4, s5, s6))

    l_w.wait()
    w_s.wait_recv()
    for cp in (wa2_o1, wa2_o2, wb2_o1, wb2_o2, *g_s):
        cp.wait_recv()

    def tile(i, carry):
        cols = pl.ds(pl.multiple_of(i * 256, 256), 256)
        acc = jnp.dot(ubd[...], asel[:, cols], preferred_element_type=F32)
        lhs = jnp.concatenate([gf[s, ch] for s in range(8) for ch in range(2)], axis=1)
        rhs = jnp.concatenate([wf[s, ch, cols, :] for s in range(8) for ch in range(2)], axis=1)
        acc += lax.dot_general(lhs, rhs, NT, preferred_element_type=F32)
        hgv[:, cols] = acc.astype(BF)
        return carry

    lax.fori_loop(0, 4, tile, 0)
    o_h = lcopy(hgv, hg_hbm)

    for ch, (cps, (o1, o2, e, ag, snd, r1, r2, own, dns, dev)) in enumerate(zip(lasts, rings)):
        for cp in cps:
            cp.wait_recv()
        tot = 2.0 * (own[...] + r2[0:128, :].astype(F32) + r2[128:256, :].astype(F32))
        for q in range(8):
            gav[q, ch * 16:(ch + 1) * 16, :] = tot[q * 16:(q + 1) * 16, 0:1024]
            gbv[q, ch] = tot[q * 16:(q + 1) * 16, 1024:1152]
    o_a = lcopy(gav, ga_hbm)
    o_b = lcopy(gbv, gb_hbm)
    for cp in pending:
        cp.wait_send()
    o_h.wait()
    o_a.wait()
    o_b.wait()


def per_device(
    hidden_input,
    key_value_gradient,
    key_value_weight,
    down_adapters,
    up_adapters,
    adapter_inner_saved,
    block_owner_tenant,
    live_block_counts,
    tenant_position,
):
    hbm = pl.BlockSpec(memory_space=pltpu.HBM)
    smem = pl.BlockSpec(memory_space=pltpu.SMEM)
    v = pltpu.VMEM
    return pl.pallas_call(
        comm_kernel,
        out_shape=(
            jax.ShapeDtypeStruct((1024, 1024), BF),
            jax.ShapeDtypeStruct((8, 32, 1024), F32),
            jax.ShapeDtypeStruct((8, 2, 16, 128), F32),
        ),
        in_specs=[hbm] * 6 + [smem] * 3,
        out_specs=(hbm, hbm, hbm),
        scratch_shapes=[
            v((8, 2, 1024, 128), BF),
            v((8, 2, 1024, 128), BF),
            v((1024, 1024), BF),
            v((128, 32, 1024), BF),
            v((128, 32, 128), BF),
            v((32, 1024), BF),
            v((2, 1024, 128), BF),
            v((2, 32, 512), F32),
            v((32, 512), F32),
            v((4, 32, 512), BF),
            v((2, 32, 512), BF),
            v((1024, 256), BF),
            v((256, 1024), BF),
            v((4, 8, 128), jnp.int32),
            v((4, 8, 128), jnp.int32),
            v((512, 512), BF),
            v((512, 512), BF),
            v((512, 1152), BF),
            v((512, 1152), BF),
            v((512, 1152), BF),
            v((512, 1152), BF),
            v((128, 1152), BF),
            v((128, 1152), BF),
            v((256, 1152), BF),
            v((256, 1152), BF),
            v((128, 1152), F32),
            v((128, 1152), F32),
            v((128, 1152), F32),
            v((128, 1152), F32),
            v((1024, 1024), BF),
            v((8, 32, 1024), F32),
            v((8, 2, 16, 128), F32),
            pltpu.SemaphoreType.DMA((N_REMOTE,)),
            pltpu.SemaphoreType.DMA((N_REMOTE,)),
            pltpu.SemaphoreType.DMA((N_LOCAL,)),
        ],
        compiler_params=pltpu.CompilerParams(
            collective_id=0, has_side_effects=True, vmem_limit_bytes=56 * 1024 * 1024
        ),
        name="projection_backward",
    )(
        hidden_input, key_value_gradient, key_value_weight, down_adapters,
        up_adapters.reshape(128, 32, 128), adapter_inner_saved,
        block_owner_tenant, live_block_counts, tenant_position,
    )


def solution(mesh):
    return jax.shard_map(
        per_device,
        mesh=mesh,
        in_specs=(
            P("dp", None),
            P(None, "dp", "tensor"),
            P(None, None, "tensor"),
            P(None, None, "tensor"),
            P(None, None, None, "tensor"),
            P(None, "dp"),
            P("dp"),
            P("dp"),
            P(),
        ),
        out_specs=(P("dp", "tensor"), P("dp", None, "tensor"), P("dp", None, None, "tensor")),
        check_vma=False,
    )
```

time: 340 us -> 62.9 us (0.18)
  waiting for transfers between devices: 278 us -> 0 us
  Pallas kernels: 0 us -> 55.9 us
  matrix products: 25.9 us -> 0 us
  between operations: 15.2 us -> 1.31 us
  other arithmetic: 9.03 us -> 0 us
  local copies, waits for them, and re-layouts: 11.2 us -> 4.81 us
    unnamed x4 -> x0, waiting for transfers between devices: 131 us -> none
    reduce_scatter x1 -> x0, waiting for transfers between devices: 89.8 us -> none  [per_device(): lax.psum_scatter(partial_value.astype(jnp.bfloat16), 'tensor', scatter_di...]
    psum x1 -> x0, waiting for transfers between devices: 57.1 us -> none  [per_device(): lax.psum(inner_part.reshape(tok_rows, rank_row_slice).astype(jnp.bfloat16...]
    pallas_call x0 -> x1, Pallas kernels: none -> 55.9 us  [per_device(): pl.pallas_call(comm_kernel, out_shape=(jax.ShapeDtypeStruct((1024, 1024),...]
    dot_general x6 -> x0, matrix products: 25.9 us -> none  [the longest x1 10.8 us: per_device(): jnp.einsum('cnj,cdj->nd', grad, key_value_weight, preferred_element_type=...]
    convert_element_type x3 -> x0, other arithmetic: 6.11 us -> none  [the longest x1 4.96 us: per_device(): (base_offset + 2.0 * adapter_input_gradient).astype(jnp.bfloat16)]
    gather x2 -> x0, local copies, waits for them, and re-layouts: 4.56 us -> none  [the longest x1 3.99 us: per_device(): selected_down = jnp.take(down_adapters, block_owner_tenant, axis=0)]
  transfers between devices with their start and end apart: 3 -> 0, of which waited for: 3 -> 0; matrix products, arithmetic and copies ran while one was open for 7% -> 0% of each run, Pallas kernels for 0% -> 0%
where the time goes in v1:
time: 62.9 us; the launch traced here: 62 us
  Pallas kernels  55.9 us (89%)
  local copies, waits for them, and re-layouts  4.81 us (8%)
  between operations  1.31 us (2%)
    pallas_call x1, Pallas kernels, per_device(): pl.pallas_call(comm_kernel, out_shape=(jax.ShapeDtypeStruct((1024, 1024),...  55.9 us
    unnamed x7, local copies, waits for them, and re-layouts  4.81 us

profile of v1, /device:TPU:1, one launch (start us, length us, event | category | flops | bytes accessed | tf_op | source)
XLA Modules:
  0.0 62.0 jit_solution(11881471874728583122)
XLA Ops:
  1.3 55.9 %projection_backward.1 = (bf16[1024,1024]{1,0:T(8,128)(2,1)}, f32[8,32,1024]{2,1,0:T(8,128)}, f32[8,2,16,128]{3,2,1,0:T(8,128)}) custom-call(bf16[1024,8192]{1,0:T(8,128)(2,1)} %x_hbm.1, bf16[2,1024,128]{2,1,0:T(8,128)(2,1)} %kvg_hbm.1, bf16[2,8192,128]{2,1,0:T(8,128)(2,1)} %w_hbm.1, bf16[128,32,1024]{2,1,0:T(8,128)(2,1)} %down_hbm.1, ...), custom_call_target="tpu_custom_call" | custom-call | tf_op jit(solution)/shard_map/projection_backward/pallas_call | solution.py:328
  57.2 0.0 copy-start
  57.2 0.0 copy-start.1
  57.2 3.2 %copy.16 = bf16[1024,1024]{1,0:T(8,128)(2,1)} copy(bf16[1024,1024]{1,0:T(8,128)(2,1)} %get-tuple-element.6) | data formatting | bytes 4194304
  60.4 0.0 copy-done
  60.4 1.0 %copy.17 = f32[8,32,1024]{2,1,0:T(8,128)} copy(f32[8,32,1024]{2,1,0:T(8,128)S(1)} %copy-done) | data formatting | bytes 2097152
  61.3 0.0 copy-done.1
  61.3 0.7 %copy.18 = f32[8,2,16,128]{3,2,1,0:T(8,128)} copy(f32[8,2,16,128]{3,2,1,0:T(8,128)S(1)} %copy-done.1) | data formatting | bytes 262144
Async XLA Ops:
  57.2 3.2 %copy-start = (f32[8,32,1024]{2,1,0:T(8,128)S(1)}, f32[8,32,1024]{2,1,0:T(8,128)}, u32[]{:S(2)}) copy-start(f32[8,32,1024]{2,1,0:T(8,128)} %get-tuple-element.7) | copy-start | bytes 3145732
  57.2 4.2 %copy-start.1 = (f32[8,2,16,128]{3,2,1,0:T(8,128)S(1)}, f32[8,2,16,128]{3,2,1,0:T(8,128)}, u32[]{:S(2)}) copy-start(f32[8,2,16,128]{3,2,1,0:T(8,128)} %get-tuple-element.8) | copy-start | bytes 393220

commit v2 on v1

--- a/solution.py
+++ b/solution.py
@@ -9,18 +9,18 @@
 BF = jnp.bfloat16
 F32 = jnp.float32
 NT = (((1,), (1,)), ((), ()))
-N_REMOTE = 80
-N_LOCAL = 12
+N_REMOTE = 100
+N_LOCAL = 6
 
 
 def comm_kernel(
     x_hbm, kvg_hbm, w_hbm, down_hbm, up_hbm, inner_hbm, owner_ref, live_ref, tp_ref,
-    hg_hbm, ga_hbm, gb_hbm,
+    hg_out, ga_out, gb_out,
     gf, wf, xv, downv, upv, innerv, kvgv,
     upart, urecv, uz, ubf, ubd, asel,
     meta_a, meta_b, ea, eb, aga, agb,
     snd_a, snd_b, r1_a, r1_b, r2_a, r2_b, own_a, own_b, dns_a, dns_b,
-    hgv, gav, gbv,
+    acc,
     ss, rs, ls,
 ):
     dp = lax.axis_index("dp")
@@ -85,7 +85,7 @@
     qa = y * 4 + x
     qb = x * 4 + y
     w1 = []
-    for d in (1, 2, 3):
+    for d in (1, 3, 2):
         for rel in (0, 1):
             slot = (4 - d) * 2 + rel
             q = qa if slot < 5 else qb
@@ -127,24 +127,30 @@
     u1.wait_recv()
     uz[0] = (upart[c] + urecv[...]).astype(BF)
     u2 = [rcopy(uz.at[0], uz.at[4 - d], zdev(d, 0)) for d in (1, 3, 2)]
-    g_r = rcopy(gf.at[0], gf.at[6], zdev(1, 0))
-    g_l = rcopy(gf.at[0], gf.at[2], zdev(3, 0))
+    first, last = pl.ds(0, 512), pl.ds(512, 512)
+
+    def gsend(slot, dst, part, dev):
+        return rcopy(gf.at[slot, :, part, :], gf.at[dst, :, part, :], dev)
+
+    g_r1 = gsend(0, 6, first, zdev(1, 0))
+    g_l1 = gsend(0, 2, last, zdev(3, 0))
+    g_r2 = gsend(0, 6, last, zdev(1, 0))
+    g_l2 = gsend(0, 2, first, zdev(3, 0))
     g_s = [rcopy(gf.at[0], gf.at[1], sib)]
 
+    half_a, half_b = pl.ds(2, 3), pl.ds(5, 3)
+
+    def wsend(half, row, size, devs):
+        part = wf.at[half, :, pl.ds(row, size), :]
+        return [rcopy(part, part, dev) for dev in devs]
+
+    xs, ys = (xdev(1), xdev(3)), (ydev(1), ydev(3))
     for cp in w1:
         cp.wait_recv()
-    half_a, half_b = pl.ds(2, 3), pl.ds(5, 3)
-
-    def wslice(half, row, size):
-        return wf.at[half, :, pl.ds(row, size), :]
-
-    def own_send(half, row, size, dev):
-        return rcopy(wslice(half, row, size), wslice(half, row, size), dev)
-
-    wa_r = own_send(half_a, qa * 64, 64, xdev(1))
-    wa_l = own_send(half_a, qa * 64, 64, xdev(3))
-    wb_r = own_send(half_b, qb * 64, 64, ydev(1))
-    wb_l = own_send(half_b, qb * 64, 64, ydev(3))
+    wa1 = wsend(half_a, qa * 64, 64, xs)
+    wb1 = wsend(half_b, qb * 64, 64, ys)
+    w2a = wsend(half_a, qa * 64, 64, ys)
+    w2b = wsend(half_b, qb * 64, 64, xs)
     w_s = rcopy(w_hbm.at[:, pl.ds(sib[1] * 1024, 1024), :], wf.at[1], sib)
 
     for cp in u2:
@@ -154,19 +160,8 @@
     ).astype(BF)
     u3 = rcopy(ubf.at[c], ubf.at[c], sib)
 
-    xl, xr = (x + 3) % 4, (x + 1) % 4
-    yd, yu = (y + 3) % 4, (y + 1) % 4
-    wa_r.wait_recv()
-    wa_l.wait_recv()
-    wa_o1 = own_send(half_a, (y * 4 + xl) * 64, 32, xdev(1))
-    wa_o2 = own_send(half_a, (y * 4 + xr) * 64 + 32, 32, xdev(3))
-    wb_r.wait_recv()
-    wb_l.wait_recv()
-    wb_o1 = own_send(half_b, (x * 4 + yd) * 64, 32, ydev(1))
-    wb_o2 = own_send(half_b, (x * 4 + yu) * 64 + 32, 32, ydev(3))
-
+    l_x.wait()
     u3.wait_recv()
-    l_x.wait()
     for b in range(8):
         ub = ubf[b // 4, :, (b % 4) * 128:(b % 4 + 1) * 128]
         term = jnp.dot(ub, xv[b * 128:(b + 1) * 128, :], preferred_element_type=F32).astype(BF)
@@ -181,14 +176,16 @@
     b_r = rcopy(row(agb, 0, 128), row(agb, 384, 128), ydev(1))
     b_l = rcopy(row(agb, 0, 128), row(agb, 128, 128), ydev(3))
 
-    wa_o1.wait_recv()
-    wa_o2.wait_recv()
-    wa2_r = own_send(half_a, y * 256, 256, ydev(1))
-    wa2_l = own_send(half_a, y * 256, 256, ydev(3))
-    wb_o1.wait_recv()
-    wb_o2.wait_recv()
-    wb2_r = own_send(half_b, x * 256, 256, xdev(1))
-    wb2_l = own_send(half_b, x * 256, 256, xdev(3))
+    xl, xr, xo = (x + 3) % 4, (x + 1) % 4, (x + 2) % 4
+    yd, yu, yo = (y + 3) % 4, (y + 1) % 4, (y + 2) % 4
+    for cp in wa1 + wb1:
+        cp.wait_recv()
+    wa1o = wsend(half_a, (y * 4 + xl) * 64, 32, xs[:1])
+    wa1o += wsend(half_a, (y * 4 + xr) * 64 + 32, 32, xs[1:])
+    wb1o = wsend(half_b, (x * 4 + yd) * 64, 32, ys[:1])
+    wb1o += wsend(half_b, (x * 4 + yu) * 64 + 32, 32, ys[1:])
+    w2a += wsend(half_a, (y * 4 + xl) * 64, 64, ys)
+    w2b += wsend(half_b, (x * 4 + yd) * 64, 64, xs)
 
     for cp in m1:
         cp.wait_recv()
@@ -217,6 +214,43 @@
             parts.append(jnp.zeros(((7 - b) * 32, 128), F32))
         ubd[b * 128:(b + 1) * 128, :] = jnp.concatenate(parts, axis=0).T.astype(BF)
 
+    def product(slots, tile):
+        start = pl.multiple_of(tile * 256, 256)
+        pairs = [(s, ch) for s in slots for ch in range(2)]
+        lhs = jnp.concatenate([gf[s, ch] for s, ch in pairs], axis=1)
+        rhs = jnp.concatenate([wf[s, ch, pl.ds(start, 256), :] for s, ch in pairs], axis=1)
+        return lax.dot_general(lhs, rhs, NT, preferred_element_type=F32)
+
+    l_w.wait()
+    w_s.wait_recv()
+    g_s[0].wait_recv()
+
+    def own_pass(i, carry):
+        cols = pl.ds(pl.multiple_of(i * 256, 256), 256)
+        acc[i] = product((0, 1), i) + jnp.dot(
+            ubd[...], asel[:, cols], preferred_element_type=F32
+        )
+        return carry
+
+    lax.fori_loop(0, 4, own_pass, 0)
+
+    g_r1.wait_recv()
+    g_l1.wait_recv()
+    g_o = [gsend(6, 4, first, zdev(1, 0)), gsend(2, 4, last, zdev(3, 0))]
+    w3 = []
+    for d in (1, 3, 2):
+        for rel in (0, 1):
+            slot = (4 - d) * 2 + rel
+            far = (yo if slot < 5 else xo) * 256
+            dst_t = ((z + d) % 4) * 2 + (c + rel) % 2
+            w3.append(
+                rcopy(
+                    w_hbm.at[:, pl.ds(dst_t * 1024 + far, 256), :],
+                    wf.at[slot, :, pl.ds(far, 256), :],
+                    zdev(d, rel),
+                )
+            )
+
     a_r.wait_recv()
     a_l.wait_recv()
     a_o1 = rcopy(row(aga, 384, 64), row(aga, 256, 64), xdev(1))
@@ -225,26 +259,22 @@
     b_l.wait_recv()
     b_o1 = rcopy(row(agb, 384, 64), row(agb, 256, 64), ydev(1))
     b_o2 = rcopy(row(agb, 192, 64), row(agb, 320, 64), ydev(3))
-
-    first, last = pl.ds(0, 512), pl.ds(512, 512)
-    g_r.wait_recv()
-    g_l.wait_recv()
-    g_o1 = rcopy(gf.at[6, :, first, :], gf.at[4, :, first, :], zdev(1, 0))
-    g_o2 = rcopy(gf.at[2, :, last, :], gf.at[4, :, last, :], zdev(3, 0))
+    w2a += wsend(half_a, (y * 4 + xr) * 64, 64, ys)
+    w2b += wsend(half_b, (x * 4 + yu) * 64, 64, xs)
+    for cp in wa1o + wb1o:
+        cp.wait_recv()
+    w2a += wsend(half_a, (y * 4 + xo) * 64, 64, ys)
+    w2b += wsend(half_b, (x * 4 + yo) * 64, 64, xs)
+    g_r2.wait_recv()
+    g_l2.wait_recv()
     g_s.append(rcopy(gf.at[6], gf.at[7], sib))
     g_s.append(rcopy(gf.at[2], gf.at[3], sib))
-
-    wa2_r.wait_recv()
-    wa2_l.wait_recv()
-    wa2_o1 = own_send(half_a, yd * 256, 128, ydev(1))
-    wa2_o2 = own_send(half_a, yu * 256 + 128, 128, ydev(3))
-    wb2_r.wait_recv()
-    wb2_l.wait_recv()
-    wb2_o1 = own_send(half_b, xl * 256, 128, xdev(1))
-    wb2_o2 = own_send(half_b, xr * 256 + 128, 128, xdev(3))
-
-    def gathered(e, ag, k):
-        return jnp.dot(e[k * 128:(k + 1) * 128, :], ag[...], preferred_element_type=F32)
+    for cp in g_o:
+        cp.wait_recv()
+    g_s.append(rcopy(gf.at[4], gf.at[5], sib))
+
+    def gathered(e, ag, k, n=1):
+        return jnp.dot(e[k * 128:(k + n) * 128, :], ag[...], preferred_element_type=F32)
 
     rings = ((a_o1, a_o2, ea, aga, snd_a, r1_a, r2_a, own_a, dns_a, ydev),
              (b_o1, b_o2, eb, agb, snd_b, r1_b, r2_b, own_b, dns_b, xdev))
@@ -255,60 +285,73 @@
         snd[256:384, :] = gathered(e, ag, 2).astype(BF)
         s1 = rcopy(row(snd, 256, 64), row(r1, 0, 64), dev(1))
         s2 = rcopy(row(snd, 320, 64), row(r1, 64, 64), dev(3))
-        up = gathered(e, ag, 1)
-        snd[192:256, :] = up[64:128].astype(BF)
-        dns[0:64, :] = up[0:64]
-        s3 = rcopy(row(snd, 192, 64), row(r2, 64, 64), dev(1))
+        steps.append([s1, s2])
+    for step, (o1, o2, e, ag, snd, r1, r2, own, dns, dev) in zip(steps, rings):
         dn = gathered(e, ag, 3)
         snd[384:448, :] = dn[0:64].astype(BF)
         dns[64:128, :] = dn[64:128]
-        s4 = rcopy(row(snd, 384, 64), row(r2, 128, 64), dev(3))
-        own[...] = gathered(e, ag, 0)
-        steps.append((s1, s2, s3, s4))
-    g_o1.wait_recv()
-    g_o2.wait_recv()
-    g_s.append(rcopy(gf.at[4], gf.at[5], sib))
-    lasts = []
-    for (s1, s2, s3, s4), (o1, o2, e, ag, snd, r1, r2, own, dns, dev) in zip(steps, rings):
+        low = gathered(e, ag, 0, 2)
+        own[...] = low[0:128]
+        snd[192:256, :] = low[192:256].astype(BF)
+        dns[0:64, :] = low[128:192]
+        step.append(rcopy(row(snd, 192, 64), row(r2, 64, 64), dev(1)))
+        step.append(rcopy(row(snd, 384, 64), row(r2, 128, 64), dev(3)))
+
+    group_a, group_b = (2, 3, 4), (5, 6, 7)
+
+    def near_pass(i, carry):
+        ta, tb = (y + i) % 4, (x + i) % 4
+        acc[ta] += product(group_a, ta)
+        acc[tb] += product(group_b, tb)
+        return carry
+
+    for cp in g_s[1:]:
+        cp.wait_recv()
+    near_pass(0, 0)
+    for cp in w2a + w2b:
+        cp.wait_recv()
+
+    def side_pass(i, carry):
+        return near_pass(1 + 2 * i, carry)
+
+    lax.fori_loop(0, 2, side_pass, 0)
+
+    for step, (o1, o2, e, ag, snd, r1, r2, own, dns, dev) in zip(steps, rings):
+        s1, s2, s3, s4 = step
         s1.wait_recv()
         snd[128:192, :] = (dns[0:64, :] + r1[0:64, :].astype(F32)).astype(BF)
         s5 = rcopy(row(snd, 128, 64), row(r2, 0, 64), dev(1))
         s2.wait_recv()
         snd[448:512, :] = (dns[64:128, :] + r1[64:128, :].astype(F32)).astype(BF)
         s6 = rcopy(row(snd, 448, 64), row(r2, 192, 64), dev(3))
-        lasts.append((s3, s4, s5, s6))
-
-    l_w.wait()
-    w_s.wait_recv()
-    for cp in (wa2_o1, wa2_o2, wb2_o1, wb2_o2, *g_s):
-        cp.wait_recv()
-
-    def tile(i, carry):
-        cols = pl.ds(pl.multiple_of(i * 256, 256), 256)
-        acc = jnp.dot(ubd[...], asel[:, cols], preferred_element_type=F32)
-        lhs = jnp.concatenate([gf[s, ch] for s in range(8) for ch in range(2)], axis=1)
-        rhs = jnp.concatenate([wf[s, ch, cols, :] for s in range(8) for ch in range(2)], axis=1)
-        acc += lax.dot_general(lhs, rhs, NT, preferred_element_type=F32)
-        hgv[:, cols] = acc.astype(BF)
-        return carry
-
-    lax.fori_loop(0, 4, tile, 0)
-    o_h = lcopy(hgv, hg_hbm)
-
-    for ch, (cps, (o1, o2, e, ag, snd, r1, r2, own, dns, dev)) in enumerate(zip(lasts, rings)):
-        for cp in cps:
+        step += [s5, s6]
+
+    for cp in w3:
+        cp.wait_recv()
+    near_pass(2, 0)
+    for i in range(4):
+        hg_out[:, i * 256:(i + 1) * 256] = acc[i].astype(BF)
+
+    for ch, (step, (o1, o2, e, ag, snd, r1, r2, own, dns, dev)) in enumerate(zip(steps, rings)):
+        for cp in step[2:]:
             cp.wait_recv()
         tot = 2.0 * (own[...] + r2[0:128, :].astype(F32) + r2[128:256, :].astype(F32))
         for q in range(8):
-            gav[q, ch * 16:(ch + 1) * 16, :] = tot[q * 16:(q + 1) * 16, 0:1024]
-            gbv[q, ch] = tot[q * 16:(q + 1) * 16, 1024:1152]
-    o_a = lcopy(gav, ga_hbm)
-    o_b = lcopy(gbv, gb_hbm)
+            ga_out[q, ch * 16:(ch + 1) * 16, :] = tot[q * 16:(q + 1) * 16, 0:1024]
+            gb_out[q, ch] = tot[q * 16:(q + 1) * 16, 1024:1152]
     for cp in pending:
         cp.wait_send()
-    o_h.wait()
-    o_a.wait()
-    o_b.wait()
+
+
+def store_kernel(hg, ga, gb, hg_hbm, ga_hbm, gb_hbm, sems):
+    copies = [
+        pltpu.make_async_copy(src, dst, sems.at[k])
+        for k, (src, dst) in enumerate(((hg, hg_hbm), (ga, ga_hbm), (gb, gb_hbm)))
+    ]
+    for cp in copies:
+        cp.start()
+    for cp in copies:
+        cp.wait()
 
 
 def per_device(
@@ -325,15 +368,18 @@
     hbm = pl.BlockSpec(memory_space=pltpu.HBM)
     smem = pl.BlockSpec(memory_space=pltpu.SMEM)
     v = pltpu.VMEM
-    return pl.pallas_call(
+    vmem = pl.BlockSpec(memory_space=pltpu.VMEM)
+    vs = (pltpu.VMEM((1024, 1024), BF), pltpu.VMEM((8, 32, 1024), F32), pltpu.VMEM((8, 2, 16, 128), F32))
+    shapes = (
+        jax.ShapeDtypeStruct((1024, 1024), BF),
+        jax.ShapeDtypeStruct((8, 32, 1024), F32),
+        jax.ShapeDtypeStruct((8, 2, 16, 128), F32),
+    )
+    outs = pl.pallas_call(
         comm_kernel,
-        out_shape=(
-            jax.ShapeDtypeStruct((1024, 1024), BF),
-            jax.ShapeDtypeStruct((8, 32, 1024), F32),
-            jax.ShapeDtypeStruct((8, 2, 16, 128), F32),
-        ),
+        out_shape=vs,
         in_specs=[hbm] * 6 + [smem] * 3,
-        out_specs=(hbm, hbm, hbm),
+        out_specs=(vmem, vmem, vmem),
         scratch_shapes=[
             v((8, 2, 1024, 128), BF),
             v((8, 2, 1024, 128), BF),
@@ -364,15 +410,13 @@
             v((128, 1152), F32),
             v((128, 1152), F32),
             v((128, 1152), F32),
-            v((1024, 1024), BF),
-            v((8, 32, 1024), F32),
-            v((8, 2, 16, 128), F32),
+            v((4, 1024, 256), F32),
             pltpu.SemaphoreType.DMA((N_REMOTE,)),
             pltpu.SemaphoreType.DMA((N_REMOTE,)),
             pltpu.SemaphoreType.DMA((N_LOCAL,)),
         ],
         compiler_params=pltpu.CompilerParams(
-            collective_id=0, has_side_effects=True, vmem_limit_bytes=56 * 1024 * 1024
+            collective_id=0, has_side_effects=True, vmem_limit_bytes=54 * 1024 * 1024
         ),
         name="projection_backward",
     )(
@@ -380,6 +424,14 @@
         up_adapters.reshape(128, 32, 128), adapter_inner_saved,
         block_owner_tenant, live_block_counts, tenant_position,
     )
+    return pl.pallas_call(
+        store_kernel,
+        out_shape=shapes,
+        in_specs=[pl.BlockSpec(memory_space=pl.ANY)] * 3,
+        out_specs=(hbm, hbm, hbm),
+        scratch_shapes=[pltpu.SemaphoreType.DMA((3,))],
+        name="store_outputs",
+    )(*[pltpu.with_memory_space_constraint(o, pltpu.VMEM) for o in outs])
 
 
 def solution(mesh):

time: 62.9 us -> 52.5 us (0.83); the launches traced: 62 us -> 52.4 us
  local copies, waits for them, and re-layouts: 4.81 us -> 0 us
  Pallas kernels: 55.9 us -> 51.1 us
    unnamed x7 -> x0, local copies, waits for them, and re-layouts: 4.81 us -> none
    pallas_call x1 -> x2, Pallas kernels: 55.9 us -> 51.1 us  [the longest x1 49.4 us: per_device(): pl.pallas_call(comm_kernel, out_shape=vs, in_specs=[hbm] * 6 + [smem] * 3...]
where the time goes in v2:
time: 52.5 us; the launch traced here: 52.4 us
  Pallas kernels  51.1 us (97%)
  between operations  1.29 us (2%)
    pallas_call x1, Pallas kernels, per_device(): pl.pallas_call(comm_kernel, out_shape=vs, in_specs=[hbm] * 6 + [smem] * 3...  49.4 us
    pallas_call x1, Pallas kernels, per_device(): pl.pallas_call(store_kernel, out_shape=shapes, in_specs=[pl.BlockSpec(mem...  1.72 us

profile of v2, /device:TPU:1, one launch (start us, length us, event | category | flops | bytes accessed | tf_op | source)
XLA Modules:
  0.0 52.4 jit_solution(9622863572639296993)
XLA Ops:
  1.3 49.4 %projection_backward.1 = (bf16[1024,1024]{1,0:T(8,128)(2,1)S(1)}, f32[8,32,1024]{2,1,0:T(8,128)S(1)}, f32[8,2,16,128]{3,2,1,0:T(8,128)S(1)}) custom-call(bf16[1024,8192]{1,0:T(8,128)(2,1)} %x_hbm.1, bf16[2,1024,128]{2,1,0:T(8,128)(2,1)} %kvg_hbm.1, bf16[2,8192,128]{2,1,0:T(8,128)(2,1)} %w_hbm.1, bf16[128,32,1024]{2,1,0:T(8,128)(2,1)} %down_hbm.1, ...), custom_call_target="tpu_custom_call" | custom-call | tf_op jit(solution)/shard_map/projection_backward/pallas_call | solution.py:378
  50.7 1.7 %store_outputs.1 = (bf16[1024,1024]{1,0:T(8,128)(2,1)}, f32[8,32,1024]{2,1,0:T(8,128)}, f32[8,2,16,128]{3,2,1,0:T(8,128)}) custom-call(bf16[1024,1024]{1,0:T(8,128)(2,1)S(1)} %get-tuple-element.6.hg, f32[8,32,1024]{2,1,0:T(8,128)S(1)} %get-tuple-element.7.ga, f32[8,2,16,128]{3,2,1,0:T(8,128)S(1)} %get-tuple-element.8.gb), custom_call_target="tpu_custom_call" | custom-call | tf_op jit(solution)/shard_map/store_outputs/pallas_call | solution.py:427

commit v3 on v2

--- a/solution.py
+++ b/solution.py
@@ -69,9 +69,6 @@
     l_kvg = lcopy(kvg_hbm, kvgv)
     l_up = lcopy(up_hbm, upv)
     l_inner = lcopy(inner_hbm, innerv)
-    l_w = lcopy(w_hbm.at[:, pl.ds(t * 1024, 1024), :], wf.at[0])
-    l_x = lcopy(x_hbm.at[:, pl.ds(t * 1024, 1024)], xv)
-    l_down = lcopy(down_hbm, downv)
 
     lane = lax.broadcasted_iota(jnp.int32, (8, 128), 1)
     pos = jnp.zeros((8, 128), jnp.int32)
@@ -101,20 +98,27 @@
     for d in (1, 2, 3):
         m1.append(rcopy(meta_a.at[0], meta_a.at[4 - d], xdev(d)))
         m1.append(rcopy(meta_b.at[0], meta_b.at[4 - d], ydev(d)))
+    l_x = lcopy(x_hbm.at[:, pl.ds(t * 1024, 1024)], xv)
 
     l_kvg.wait()
     l_up.wait()
     live = live_ref[0]
+    off = jnp.zeros((16, 128), BF)
     for b in range(8):
         rows = pl.ds(b * 128, 128)
         upb = upv[owner_ref[b]]
+        up2 = jnp.concatenate(
+            [jnp.concatenate([upb[0:16], off], axis=1), jnp.concatenate([off, upb[16:32]], axis=1)],
+            axis=0,
+        )
+        g2 = []
         for ch in range(2):
             g = kvgv[ch, rows, :]
-            g = jnp.where(b < live, g, jnp.zeros_like(g))
-            gf[0, ch, rows, :] = g
-            upart[b // 4, ch * 16:(ch + 1) * 16, (b % 4) * 128:(b % 4 + 1) * 128] = (
-                lax.dot_general(upb[ch * 16:(ch + 1) * 16], g, NT, preferred_element_type=F32)
-            )
+            g2.append(jnp.where(b < live, g, jnp.zeros_like(g)))
+            gf[0, ch, rows, :] = g2[ch]
+        upart[b // 4, :, (b % 4) * 128:(b % 4 + 1) * 128] = lax.dot_general(
+            up2, jnp.concatenate(g2, axis=1), NT, preferred_element_type=F32
+        )
     u1 = rcopy(upart.at[1 - c], urecv, sib)
     l_inner.wait()
     for b in range(8):
@@ -124,6 +128,21 @@
                 innerv[ch * 16:(ch + 1) * 16, b * 128:(b + 1) * 128], gf[0, ch, rows, :],
                 preferred_element_type=F32,
             ).astype(BF)
+
+    def wsend(slots, row, size, devs):
+        part = wf.at[slots, :, pl.ds(row, size), :]
+        return [rcopy(part, part, dev) for dev in devs]
+
+    xs, ys = (xdev(1), xdev(3)), (ydev(1), ydev(3))
+    half_a, half_b = pl.ds(2, 3), pl.ds(5, 3)
+    wa1, wb1, w2a, w2b = [], [], [], []
+
+    def start_rings(slots_a, slots_b):
+        wa1.extend(wsend(slots_a, qa * 64, 64, xs))
+        wb1.extend(wsend(slots_b, qb * 64, 64, ys))
+        w2a.extend(wsend(slots_a, qa * 64, 64, ys))
+        w2b.extend(wsend(slots_b, qb * 64, 64, xs))
+
     u1.wait_recv()
     uz[0] = (upart[c] + urecv[...]).astype(BF)
     u2 = [rcopy(uz.at[0], uz.at[4 - d], zdev(d, 0)) for d in (1, 3, 2)]
@@ -136,22 +155,14 @@
     g_l1 = gsend(0, 2, last, zdev(3, 0))
     g_r2 = gsend(0, 6, last, zdev(1, 0))
     g_l2 = gsend(0, 2, first, zdev(3, 0))
-    g_s = [rcopy(gf.at[0], gf.at[1], sib)]
-
-    half_a, half_b = pl.ds(2, 3), pl.ds(5, 3)
-
-    def wsend(half, row, size, devs):
-        part = wf.at[half, :, pl.ds(row, size), :]
-        return [rcopy(part, part, dev) for dev in devs]
-
-    xs, ys = (xdev(1), xdev(3)), (ydev(1), ydev(3))
-    for cp in w1:
-        cp.wait_recv()
-    wa1 = wsend(half_a, qa * 64, 64, xs)
-    wb1 = wsend(half_b, qb * 64, 64, ys)
-    w2a = wsend(half_a, qa * 64, 64, ys)
-    w2b = wsend(half_b, qb * 64, 64, xs)
-    w_s = rcopy(w_hbm.at[:, pl.ds(sib[1] * 1024, 1024), :], wf.at[1], sib)
+    for cp in w1[:4]:
+        cp.wait_recv()
+    start_rings(pl.ds(2, 2), pl.ds(6, 2))
+    for cp in w1[4:]:
+        cp.wait_recv()
+    start_rings(pl.ds(4, 1), pl.ds(5, 1))
+    l_w = lcopy(w_hbm.at[:, pl.ds(t * 1024, 1024), :], wf.at[0])
+    l_down = lcopy(down_hbm, downv)
 
     for cp in u2:
         cp.wait_recv()
@@ -171,10 +182,15 @@
     def row(ref, start, size):
         return ref.at[pl.ds(start, size), :]
 
-    a_r = rcopy(row(aga, 0, 128), row(aga, 384, 128), xdev(1))
-    a_l = rcopy(row(aga, 0, 128), row(aga, 128, 128), xdev(3))
-    b_r = rcopy(row(agb, 0, 128), row(agb, 384, 128), ydev(1))
-    b_l = rcopy(row(agb, 0, 128), row(agb, 128, 128), ydev(3))
+    ag_1, ag_2 = [], []
+    for ag, dev in ((aga, xdev), (agb, ydev)):
+        ag_1.append(rcopy(row(ag, 0, 64), row(ag, 384, 64), dev(1)))
+        ag_1.append(rcopy(row(ag, 64, 64), row(ag, 192, 64), dev(3)))
+    for ag, dev in ((aga, xdev), (agb, ydev)):
+        ag_2.append(rcopy(row(ag, 64, 64), row(ag, 448, 64), dev(1)))
+        ag_2.append(rcopy(row(ag, 0, 64), row(ag, 128, 64), dev(3)))
+    g_s = [rcopy(gf.at[0], gf.at[1], sib)]
+    w_s = rcopy(w_hbm.at[:, pl.ds(sib[1] * 1024, 1024), :], wf.at[1], sib)
 
     xl, xr, xo = (x + 3) % 4, (x + 1) % 4, (x + 2) % 4
     yd, yu, yo = (y + 3) % 4, (y + 1) % 4, (y + 2) % 4
@@ -184,8 +200,6 @@
     wa1o += wsend(half_a, (y * 4 + xr) * 64 + 32, 32, xs[1:])
     wb1o = wsend(half_b, (x * 4 + yd) * 64, 32, ys[:1])
     wb1o += wsend(half_b, (x * 4 + yu) * 64 + 32, 32, ys[1:])
-    w2a += wsend(half_a, (y * 4 + xl) * 64, 64, ys)
-    w2b += wsend(half_b, (x * 4 + yd) * 64, 64, xs)
 
     for cp in m1:
         cp.wait_recv()
@@ -213,26 +227,6 @@
         if b < 7:
             parts.append(jnp.zeros(((7 - b) * 32, 128), F32))
         ubd[b * 128:(b + 1) * 128, :] = jnp.concatenate(parts, axis=0).T.astype(BF)
-
-    def product(slots, tile):
-        start = pl.multiple_of(tile * 256, 256)
-        pairs = [(s, ch) for s in slots for ch in range(2)]
-        lhs = jnp.concatenate([gf[s, ch] for s, ch in pairs], axis=1)
-        rhs = jnp.concatenate([wf[s, ch, pl.ds(start, 256), :] for s, ch in pairs], axis=1)
-        return lax.dot_general(lhs, rhs, NT, preferred_element_type=F32)
-
-    l_w.wait()
-    w_s.wait_recv()
-    g_s[0].wait_recv()
-
-    def own_pass(i, carry):
-        cols = pl.ds(pl.multiple_of(i * 256, 256), 256)
-        acc[i] = product((0, 1), i) + jnp.dot(
-            ubd[...], asel[:, cols], preferred_element_type=F32
-        )
-        return carry
-
-    lax.fori_loop(0, 4, own_pass, 0)
 
     g_r1.wait_recv()
     g_l1.wait_recv()
@@ -251,14 +245,34 @@
                 )
             )
 
-    a_r.wait_recv()
-    a_l.wait_recv()
+    def product(slots, tile):
+        start = pl.multiple_of(tile * 256, 256)
+        pairs = [(s, ch) for s in slots for ch in range(2)]
+        lhs = jnp.concatenate([gf[s, ch] for s, ch in pairs], axis=1)
+        rhs = jnp.concatenate([wf[s, ch, pl.ds(start, 256), :] for s, ch in pairs], axis=1)
+        return lax.dot_general(lhs, rhs, NT, preferred_element_type=F32)
+
+    l_w.wait()
+    w_s.wait_recv()
+    g_s[0].wait_recv()
+
+    def own_pass(i, carry):
+        cols = pl.ds(pl.multiple_of(i * 256, 256), 256)
+        acc[i] = product((0, 1), i) + jnp.dot(
+            ubd[...], asel[:, cols], preferred_element_type=F32
+        )
+        return carry
+
+    lax.fori_loop(0, 4, own_pass, 0)
+
+    for cp in ag_1:
+        cp.wait_recv()
     a_o1 = rcopy(row(aga, 384, 64), row(aga, 256, 64), xdev(1))
     a_o2 = rcopy(row(aga, 192, 64), row(aga, 320, 64), xdev(3))
-    b_r.wait_recv()
-    b_l.wait_recv()
     b_o1 = rcopy(row(agb, 384, 64), row(agb, 256, 64), ydev(1))
     b_o2 = rcopy(row(agb, 192, 64), row(agb, 320, 64), ydev(3))
+    w2a += wsend(half_a, (y * 4 + xl) * 64, 64, ys)
+    w2b += wsend(half_b, (x * 4 + yd) * 64, 64, xs)
     w2a += wsend(half_a, (y * 4 + xr) * 64, 64, ys)
     w2b += wsend(half_b, (x * 4 + yu) * 64, 64, xs)
     for cp in wa1o + wb1o:
@@ -269,9 +283,6 @@
     g_l2.wait_recv()
     g_s.append(rcopy(gf.at[6], gf.at[7], sib))
     g_s.append(rcopy(gf.at[2], gf.at[3], sib))
-    for cp in g_o:
-        cp.wait_recv()
-    g_s.append(rcopy(gf.at[4], gf.at[5], sib))
 
     def gathered(e, ag, k, n=1):
         return jnp.dot(e[k * 128:(k + n) * 128, :], ag[...], preferred_element_type=F32)
@@ -279,6 +290,8 @@
     rings = ((a_o1, a_o2, ea, aga, snd_a, r1_a, r2_a, own_a, dns_a, ydev),
              (b_o1, b_o2, eb, agb, snd_b, r1_b, r2_b, own_b, dns_b, xdev))
     steps = []
+    for cp in ag_2:
+        cp.wait_recv()
     for o1, o2, e, ag, snd, r1, r2, own, dns, dev in rings:
         o1.wait_recv()
         o2.wait_recv()
@@ -297,6 +310,9 @@
         step.append(rcopy(row(snd, 192, 64), row(r2, 64, 64), dev(1)))
         step.append(rcopy(row(snd, 384, 64), row(r2, 128, 64), dev(3)))
 
+    for cp in g_o:
+        cp.wait_recv()
+    g_s.append(rcopy(gf.at[4], gf.at[5], sib))
     group_a, group_b = (2, 3, 4), (5, 6, 7)
 
     def near_pass(i, carry):
@@ -344,9 +360,11 @@
 
 
 def store_kernel(hg, ga, gb, hg_hbm, ga_hbm, gb_hbm, sems):
+    parts = [(hg, hg_hbm, 256 * i, 256) for i in range(4)]
+    parts += [(ga, ga_hbm, 4 * i, 4) for i in range(2)] + [(gb, gb_hbm, 0, 8)]
     copies = [
-        pltpu.make_async_copy(src, dst, sems.at[k])
-        for k, (src, dst) in enumerate(((hg, hg_hbm), (ga, ga_hbm), (gb, gb_hbm)))
+        pltpu.make_async_copy(src.at[pl.ds(at, size)], dst.at[pl.ds(at, size)], sems.at[k])
+        for k, (src, dst, at, size) in enumerate(parts)
     ]
     for cp in copies:
         cp.start()
@@ -429,7 +447,7 @@
         out_shape=shapes,
         in_specs=[pl.BlockSpec(memory_space=pl.ANY)] * 3,
         out_specs=(hbm, hbm, hbm),
-        scratch_shapes=[pltpu.SemaphoreType.DMA((3,))],
+        scratch_shapes=[pltpu.SemaphoreType.DMA((7,))],
         name="store_outputs",
     )(*[pltpu.with_memory_space_constraint(o, pltpu.VMEM) for o in outs])
 

time: 52.5 us -> 51.6 us (0.983)
  Pallas kernels: 51.1 us -> 50.2 us
    pallas_call x1, Pallas kernels: 49.4 us -> 48.4 us  [per_device(): pl.pallas_call(comm_kernel, out_shape=vs, in_specs=[hbm] * 6 + [smem] * 3...]
where the time goes in v3:
time: 51.6 us; the launch traced here: 51.4 us
  Pallas kernels  50.2 us (97%)
  between operations  1.29 us (2%)
    pallas_call x1, Pallas kernels, per_device(): pl.pallas_call(comm_kernel, out_shape=vs, in_specs=[hbm] * 6 + [smem] * 3...  48.4 us
    pallas_call x1, Pallas kernels, per_device(): pl.pallas_call(store_kernel, out_shape=shapes, in_specs=[pl.BlockSpec(mem...  1.75 us

profile of v3, /device:TPU:1, one launch (start us, length us, event | category | flops | bytes accessed | tf_op | source)
XLA Modules:
  0.0 51.4 jit_solution(13966315884567421787)
XLA Ops:
  1.3 48.4 %projection_backward.1 = (bf16[1024,1024]{1,0:T(8,128)(2,1)S(1)}, f32[8,32,1024]{2,1,0:T(8,128)S(1)}, f32[8,2,16,128]{3,2,1,0:T(8,128)S(1)}) custom-call(bf16[1024,8192]{1,0:T(8,128)(2,1)} %x_hbm.1, bf16[2,1024,128]{2,1,0:T(8,128)(2,1)} %kvg_hbm.1, bf16[2,8192,128]{2,1,0:T(8,128)(2,1)} %w_hbm.1, bf16[128,32,1024]{2,1,0:T(8,128)(2,1)} %down_hbm.1, ...), custom_call_target="tpu_custom_call" | custom-call | tf_op jit(solution)/shard_map/projection_backward/pallas_call | solution.py:396
  49.7 1.8 %store_outputs.1 = (bf16[1024,1024]{1,0:T(8,128)(2,1)}, f32[8,32,1024]{2,1,0:T(8,128)}, f32[8,2,16,128]{3,2,1,0:T(8,128)}) custom-call(bf16[1024,1024]{1,0:T(8,128)(2,1)S(1)} %get-tuple-element.6.hg, f32[8,32,1024]{2,1,0:T(8,128)S(1)} %get-tuple-element.7.ga, f32[8,2,16,128]{3,2,1,0:T(8,128)S(1)} %get-tuple-element.8.gb), custom_call_target="tpu_custom_call" | custom-call | tf_op jit(solution)/shard_map/store_outputs/pallas_call | solution.py:445

commit v4 on v3

--- a/solution.py
+++ b/solution.py
@@ -9,7 +9,7 @@
 BF = jnp.bfloat16
 F32 = jnp.float32
 NT = (((1,), (1,)), ((), ()))
-N_REMOTE = 100
+N_REMOTE = 136
 N_LOCAL = 6
 
 
@@ -82,18 +82,17 @@
     qa = y * 4 + x
     qb = x * 4 + y
     w1 = []
-    for d in (1, 3, 2):
-        for rel in (0, 1):
-            slot = (4 - d) * 2 + rel
-            q = qa if slot < 5 else qb
-            dst_t = ((z + d) % 4) * 2 + (c + rel) % 2
-            w1.append(
-                rcopy(
-                    w_hbm.at[:, pl.ds(dst_t * 1024 + q * 64, 64), :],
-                    wf.at[slot, :, pl.ds(q * 64, 64), :],
-                    zdev(d, rel),
-                )
+    for d, rel in ((1, 0), (3, 0), (1, 1), (3, 1), (2, 0), (2, 1)):
+        slot = (4 - d) * 2 + rel
+        q = qa if slot < 5 else qb
+        dst_t = ((z + d) % 4) * 2 + (c + rel) % 2
+        w1.append(
+            rcopy(
+                w_hbm.at[:, pl.ds(dst_t * 1024 + q * 64, 64), :],
+                wf.at[slot, :, pl.ds(q * 64, 64), :],
+                zdev(d, rel),
             )
+        )
     m1 = []
     for d in (1, 2, 3):
         m1.append(rcopy(meta_a.at[0], meta_a.at[4 - d], xdev(d)))
@@ -129,6 +128,15 @@
                 preferred_element_type=F32,
             ).astype(BF)
 
+    def row(ref, start, size, cols=slice(None)):
+        return ref.at[pl.ds(start, size), cols]
+
+    low, high = pl.ds(0, 1024), pl.ds(1024, 128)
+    bg = []
+    for ag, dev in ((aga, xdev), (agb, ydev)):
+        bg.append(rcopy(row(ag, 0, 128, high), row(ag, 384, 128, high), dev(1)))
+        bg.append(rcopy(row(ag, 0, 128, high), row(ag, 128, 128, high), dev(3)))
+
     def wsend(slots, row, size, devs):
         part = wf.at[slots, :, pl.ds(row, size), :]
         return [rcopy(part, part, dev) for dev in devs]
@@ -155,9 +163,12 @@
     g_l1 = gsend(0, 2, last, zdev(3, 0))
     g_r2 = gsend(0, 6, last, zdev(1, 0))
     g_l2 = gsend(0, 2, first, zdev(3, 0))
-    for cp in w1[:4]:
-        cp.wait_recv()
-    start_rings(pl.ds(2, 2), pl.ds(6, 2))
+    for cp in w1[:2]:
+        cp.wait_recv()
+    start_rings(pl.ds(2, 1), pl.ds(6, 1))
+    for cp in w1[2:4]:
+        cp.wait_recv()
+    start_rings(pl.ds(3, 1), pl.ds(7, 1))
     for cp in w1[4:]:
         cp.wait_recv()
     start_rings(pl.ds(4, 1), pl.ds(5, 1))
@@ -179,16 +190,18 @@
         aga[b * 16:(b + 1) * 16, 0:1024] = term[0:16]
         agb[b * 16:(b + 1) * 16, 0:1024] = term[16:32]
 
-    def row(ref, start, size):
-        return ref.at[pl.ds(start, size), :]
-
     ag_1, ag_2 = [], []
     for ag, dev in ((aga, xdev), (agb, ydev)):
-        ag_1.append(rcopy(row(ag, 0, 64), row(ag, 384, 64), dev(1)))
-        ag_1.append(rcopy(row(ag, 64, 64), row(ag, 192, 64), dev(3)))
+        ag_1.append(rcopy(row(ag, 0, 64, low), row(ag, 384, 64, low), dev(1)))
+        ag_1.append(rcopy(row(ag, 64, 64, low), row(ag, 192, 64, low), dev(3)))
     for ag, dev in ((aga, xdev), (agb, ydev)):
-        ag_2.append(rcopy(row(ag, 64, 64), row(ag, 448, 64), dev(1)))
-        ag_2.append(rcopy(row(ag, 0, 64), row(ag, 128, 64), dev(3)))
+        ag_2.append(rcopy(row(ag, 64, 64, low), row(ag, 448, 64, low), dev(1)))
+        ag_2.append(rcopy(row(ag, 0, 64, low), row(ag, 128, 64, low), dev(3)))
+    for cp in bg:
+        cp.wait_recv()
+    for ag, dev in ((aga, xdev), (agb, ydev)):
+        ag_2.append(rcopy(row(ag, 384, 64, high), row(ag, 256, 64, high), dev(1)))
+        ag_2.append(rcopy(row(ag, 192, 64, high), row(ag, 320, 64, high), dev(3)))
     g_s = [rcopy(gf.at[0], gf.at[1], sib)]
     w_s = rcopy(w_hbm.at[:, pl.ds(sib[1] * 1024, 1024), :], wf.at[1], sib)
 
@@ -196,10 +209,11 @@
     yd, yu, yo = (y + 3) % 4, (y + 1) % 4, (y + 2) % 4
     for cp in wa1 + wb1:
         cp.wait_recv()
-    wa1o = wsend(half_a, (y * 4 + xl) * 64, 32, xs[:1])
-    wa1o += wsend(half_a, (y * 4 + xr) * 64 + 32, 32, xs[1:])
-    wb1o = wsend(half_b, (x * 4 + yd) * 64, 32, ys[:1])
-    wb1o += wsend(half_b, (x * 4 + yu) * 64 + 32, 32, ys[1:])
+    far_a, far_b = pl.ds(4, 1), pl.ds(5, 1)
+    w1o = wsend(far_a, (y * 4 + xl) * 64, 32, xs[:1])
+    w1o += wsend(far_a, (y * 4 + xr) * 64 + 32, 32, xs[1:])
+    w1o += wsend(far_b, (x * 4 + yd) * 64, 32, ys[:1])
+    w1o += wsend(far_b, (x * 4 + yu) * 64 + 32, 32, ys[1:])
 
     for cp in m1:
         cp.wait_recv()
@@ -231,19 +245,29 @@
     g_r1.wait_recv()
     g_l1.wait_recv()
     g_o = [gsend(6, 4, first, zdev(1, 0)), gsend(2, 4, last, zdev(3, 0))]
+
+    def near_send(row_a, row_b, size):
+        sent = []
+        for d in (1, 3):
+            for rel in (0, 1):
+                slot = (4 - d) * 2 + rel
+                at = row_a if slot < 5 else row_b
+                dst_t = ((z + d) % 4) * 2 + (c + rel) % 2
+                sent.append(
+                    rcopy(
+                        w_hbm.at[:, pl.ds(dst_t * 1024 + at, size), :],
+                        wf.at[slot, :, pl.ds(at, size), :],
+                        zdev(d, rel),
+                    )
+                )
+        return sent
+
     w3 = []
-    for d in (1, 3, 2):
-        for rel in (0, 1):
-            slot = (4 - d) * 2 + rel
-            far = (yo if slot < 5 else xo) * 256
-            dst_t = ((z + d) % 4) * 2 + (c + rel) % 2
-            w3.append(
-                rcopy(
-                    w_hbm.at[:, pl.ds(dst_t * 1024 + far, 256), :],
-                    wf.at[slot, :, pl.ds(far, 256), :],
-                    zdev(d, rel),
-                )
-            )
+    for i in (0, 3, 1):
+        w3.append(
+            near_send((((y + i) % 4) * 4 + xo) * 64, (((x + i) % 4) * 4 + yo) * 64, 64)
+        )
+    w3.append(near_send(yo * 256, xo * 256, 256))
 
     def product(slots, tile):
         start = pl.multiple_of(tile * 256, 256)
@@ -267,18 +291,18 @@
 
     for cp in ag_1:
         cp.wait_recv()
-    a_o1 = rcopy(row(aga, 384, 64), row(aga, 256, 64), xdev(1))
-    a_o2 = rcopy(row(aga, 192, 64), row(aga, 320, 64), xdev(3))
-    b_o1 = rcopy(row(agb, 384, 64), row(agb, 256, 64), ydev(1))
-    b_o2 = rcopy(row(agb, 192, 64), row(agb, 320, 64), ydev(3))
+    a_o1 = rcopy(row(aga, 384, 64, low), row(aga, 256, 64, low), xdev(1))
+    a_o2 = rcopy(row(aga, 192, 64, low), row(aga, 320, 64, low), xdev(3))
+    b_o1 = rcopy(row(agb, 384, 64, low), row(agb, 256, 64, low), ydev(1))
+    b_o2 = rcopy(row(agb, 192, 64, low), row(agb, 320, 64, low), ydev(3))
     w2a += wsend(half_a, (y * 4 + xl) * 64, 64, ys)
     w2b += wsend(half_b, (x * 4 + yd) * 64, 64, xs)
     w2a += wsend(half_a, (y * 4 + xr) * 64, 64, ys)
     w2b += wsend(half_b, (x * 4 + yu) * 64, 64, xs)
-    for cp in wa1o + wb1o:
-        cp.wait_recv()
-    w2a += wsend(half_a, (y * 4 + xo) * 64, 64, ys)
-    w2b += wsend(half_b, (x * 4 + yo) * 64, 64, xs)
+    for cp in w1o:
+        cp.wait_recv()
+    w2a += wsend(far_a, (y * 4 + xo) * 64, 64, ys)
+    w2b += wsend(far_b, (x * 4 + yo) * 64, 64, xs)
     g_r2.wait_recv()
     g_l2.wait_recv()
     g_s.append(rcopy(gf.at[6], gf.at[7], sib))
@@ -303,10 +327,10 @@
         dn = gathered(e, ag, 3)
         snd[384:448, :] = dn[0:64].astype(BF)
         dns[64:128, :] = dn[64:128]
-        low = gathered(e, ag, 0, 2)
-        own[...] = low[0:128]
-        snd[192:256, :] = low[192:256].astype(BF)
-        dns[0:64, :] = low[128:192]
+        up = gathered(e, ag, 0, 2)
+        own[...] = up[0:128]
+        snd[192:256, :] = up[192:256].astype(BF)
+        dns[0:64, :] = up[128:192]
         step.append(rcopy(row(snd, 192, 64), row(r2, 64, 64), dev(1)))
         step.append(rcopy(row(snd, 384, 64), row(r2, 128, 64), dev(3)))
 
@@ -321,16 +345,10 @@
         acc[tb] += product(group_b, tb)
         return carry
 
-    for cp in g_s[1:]:
-        cp.wait_recv()
-    near_pass(0, 0)
     for cp in w2a + w2b:
         cp.wait_recv()
-
-    def side_pass(i, carry):
-        return near_pass(1 + 2 * i, carry)
-
-    lax.fori_loop(0, 2, side_pass, 0)
+    w2o = wsend(far_a, yd * 256, 128, ys[:1]) + wsend(far_a, yu * 256 + 128, 128, ys[1:])
+    w2o += wsend(far_b, xl * 256, 128, xs[:1]) + wsend(far_b, xr * 256 + 128, 128, xs[1:])
 
     for step, (o1, o2, e, ag, snd, r1, r2, own, dns, dev) in zip(steps, rings):
         s1, s2, s3, s4 = step
@@ -342,7 +360,18 @@
         s6 = rcopy(row(snd, 448, 64), row(r2, 192, 64), dev(3))
         step += [s5, s6]
 
-    for cp in w3:
+    for cp in g_s[1:] + w3[0]:
+        cp.wait_recv()
+    near_pass(0, 0)
+    for cp in w3[1] + w3[2]:
+        cp.wait_recv()
+
+    def side_pass(i, carry):
+        return near_pass(1 + 2 * i, carry)
+
+    lax.fori_loop(0, 2, side_pass, 0)
+
+    for cp in w3[3] + w2o:
         cp.wait_recv()
     near_pass(2, 0)
     for i in range(4):

time: 51.6 us -> 49.9 us (0.967)
  Pallas kernels: 50.2 us -> 48.5 us
    pallas_call x1, Pallas kernels: 48.4 us -> 46.7 us  [per_device(): pl.pallas_call(comm_kernel, out_shape=vs, in_specs=[hbm] * 6 + [smem] * 3...]
where the time goes in v4:
time: 49.9 us; the launch traced here: 49.8 us
  Pallas kernels  48.5 us (97%)
  between operations  1.29 us (3%)
    pallas_call x1, Pallas kernels, per_device(): pl.pallas_call(comm_kernel, out_shape=vs, in_specs=[hbm] * 6 + [smem] * 3...  46.7 us
    pallas_call x1, Pallas kernels, per_device(): pl.pallas_call(store_kernel, out_shape=shapes, in_specs=[pl.BlockSpec(mem...  1.75 us

profile of v4, /device:TPU:1, one launch (start us, length us, event | category | flops | bytes accessed | tf_op | source)
XLA Modules:
  0.0 49.8 jit_solution(5180728512796560696)
XLA Ops:
  1.3 46.7 %projection_backward.1 = (bf16[1024,1024]{1,0:T(8,128)(2,1)S(1)}, f32[8,32,1024]{2,1,0:T(8,128)S(1)}, f32[8,2,16,128]{3,2,1,0:T(8,128)S(1)}) custom-call(bf16[1024,8192]{1,0:T(8,128)(2,1)} %x_hbm.1, bf16[2,1024,128]{2,1,0:T(8,128)(2,1)} %kvg_hbm.1, bf16[2,8192,128]{2,1,0:T(8,128)(2,1)} %w_hbm.1, bf16[128,32,1024]{2,1,0:T(8,128)(2,1)} %down_hbm.1, ...), custom_call_target="tpu_custom_call" | custom-call | tf_op jit(solution)/shard_map/projection_backward/pallas_call | solution.py:425
  48.0 1.8 %store_outputs.1 = (bf16[1024,1024]{1,0:T(8,128)(2,1)}, f32[8,32,1024]{2,1,0:T(8,128)}, f32[8,2,16,128]{3,2,1,0:T(8,128)}) custom-call(bf16[1024,1024]{1,0:T(8,128)(2,1)S(1)} %get-tuple-element.6.hg, f32[8,32,1024]{2,1,0:T(8,128)S(1)} %get-tuple-element.7.ga, f32[8,2,16,128]{3,2,1,0:T(8,128)S(1)} %get-tuple-element.8.gb), custom_call_target="tpu_custom_call" | custom-call | tf_op jit(solution)/shard_map/store_outputs/pallas_call | solution.py:474

commit v5 on v4

--- a/solution.py
+++ b/solution.py
@@ -9,7 +9,7 @@
 BF = jnp.bfloat16
 F32 = jnp.float32
 NT = (((1,), (1,)), ((), ()))
-N_REMOTE = 136
+N_REMOTE = 120
 N_LOCAL = 6
 
 
@@ -371,6 +371,10 @@
 
     lax.fori_loop(0, 2, side_pass, 0)
 
+    late = [cp for step in steps for cp in step[4:]]
+    for cp in pending:
+        if all(cp is not other for other in late):
+            cp.wait_send()
     for cp in w3[3] + w2o:
         cp.wait_recv()
     near_pass(2, 0)
@@ -384,7 +388,7 @@
         for q in range(8):
             ga_out[q, ch * 16:(ch + 1) * 16, :] = tot[q * 16:(q + 1) * 16, 0:1024]
             gb_out[q, ch] = tot[q * 16:(q + 1) * 16, 1024:1152]
-    for cp in pending:
+    for cp in late:
         cp.wait_send()
 
 

time: 49.9 us -> 49.4 us (0.990)
  Pallas kernels: 48.5 us -> 48 us
where the time goes in v5:
time: 49.4 us; the launch traced here: 49.3 us
  Pallas kernels  48 us (97%)
  between operations  1.29 us (3%)
    pallas_call x1, Pallas kernels, per_device(): pl.pallas_call(comm_kernel, out_shape=vs, in_specs=[hbm] * 6 + [smem] * 3...  46.3 us
    pallas_call x1, Pallas kernels, per_device(): pl.pallas_call(store_kernel, out_shape=shapes, in_specs=[pl.BlockSpec(mem...  1.75 us

profile of v5, /device:TPU:1, one launch (start us, length us, event | category | flops | bytes accessed | tf_op | source)
XLA Modules:
  0.0 49.3 jit_solution(13334534396014702676)
XLA Ops:
  1.3 46.3 %projection_backward.1 = (bf16[1024,1024]{1,0:T(8,128)(2,1)S(1)}, f32[8,32,1024]{2,1,0:T(8,128)S(1)}, f32[8,2,16,128]{3,2,1,0:T(8,128)S(1)}) custom-call(bf16[1024,8192]{1,0:T(8,128)(2,1)} %x_hbm.1, bf16[2,1024,128]{2,1,0:T(8,128)(2,1)} %kvg_hbm.1, bf16[2,8192,128]{2,1,0:T(8,128)(2,1)} %w_hbm.1, bf16[128,32,1024]{2,1,0:T(8,128)(2,1)} %down_hbm.1, ...), custom_call_target="tpu_custom_call" | custom-call | tf_op jit(solution)/shard_map/projection_backward/pallas_call | solution.py:429
  47.6 1.8 %store_outputs.1 = (bf16[1024,1024]{1,0:T(8,128)(2,1)}, f32[8,32,1024]{2,1,0:T(8,128)}, f32[8,2,16,128]{3,2,1,0:T(8,128)}) custom-call(bf16[1024,1024]{1,0:T(8,128)(2,1)S(1)} %get-tuple-element.6.hg, f32[8,32,1024]{2,1,0:T(8,128)S(1)} %get-tuple-element.7.ga, f32[8,2,16,128]{3,2,1,0:T(8,128)S(1)} %get-tuple-element.8.gb), custom_call_target="tpu_custom_call" | custom-call | tf_op jit(solution)/shard_map/store_outputs/pallas_call | solution.py:478

commit v6 on v5

--- a/solution.py
+++ b/solution.py
@@ -154,6 +154,9 @@
     u1.wait_recv()
     uz[0] = (upart[c] + urecv[...]).astype(BF)
     u2 = [rcopy(uz.at[0], uz.at[4 - d], zdev(d, 0)) for d in (1, 3, 2)]
+    for cp in w1[:2]:
+        cp.wait_recv()
+    start_rings(pl.ds(2, 1), pl.ds(6, 1))
     first, last = pl.ds(0, 512), pl.ds(512, 512)
 
     def gsend(slot, dst, part, dev):
@@ -163,9 +166,6 @@
     g_l1 = gsend(0, 2, last, zdev(3, 0))
     g_r2 = gsend(0, 6, last, zdev(1, 0))
     g_l2 = gsend(0, 2, first, zdev(3, 0))
-    for cp in w1[:2]:
-        cp.wait_recv()
-    start_rings(pl.ds(2, 1), pl.ds(6, 1))
     for cp in w1[2:4]:
         cp.wait_recv()
     start_rings(pl.ds(3, 1), pl.ds(7, 1))

time: 49.4 us -> 49.4 us (level)
  no operation moved by 1% of the time
where the time goes in v6:
time: 49.4 us; the launch traced here: 49.3 us
  Pallas kernels  48 us (97%)
  between operations  1.29 us (3%)
    pallas_call x1, Pallas kernels, per_device(): pl.pallas_call(comm_kernel, out_shape=vs, in_specs=[hbm] * 6 + [smem] * 3...  46.3 us
    pallas_call x1, Pallas kernels, per_device(): pl.pallas_call(store_kernel, out_shape=shapes, in_specs=[pl.BlockSpec(mem...  1.75 us

profile of v6, /device:TPU:1, one launch (start us, length us, event | category | flops | bytes accessed | tf_op | source)
XLA Modules:
  0.0 49.3 jit_solution(6621943602767071384)
XLA Ops:
  1.3 46.3 %projection_backward.1 = (bf16[1024,1024]{1,0:T(8,128)(2,1)S(1)}, f32[8,32,1024]{2,1,0:T(8,128)S(1)}, f32[8,2,16,128]{3,2,1,0:T(8,128)S(1)}) custom-call(bf16[1024,8192]{1,0:T(8,128)(2,1)} %x_hbm.1, bf16[2,1024,128]{2,1,0:T(8,128)(2,1)} %kvg_hbm.1, bf16[2,8192,128]{2,1,0:T(8,128)(2,1)} %w_hbm.1, bf16[128,32,1024]{2,1,0:T(8,128)(2,1)} %down_hbm.1, ...), custom_call_target="tpu_custom_call" | custom-call | tf_op jit(solution)/shard_map/projection_backward/pallas_call | solution.py:429
  47.6 1.8 %store_outputs.1 = (bf16[1024,1024]{1,0:T(8,128)(2,1)}, f32[8,32,1024]{2,1,0:T(8,128)}, f32[8,2,16,128]{3,2,1,0:T(8,128)}) custom-call(bf16[1024,1024]{1,0:T(8,128)(2,1)S(1)} %get-tuple-element.6.hg, f32[8,32,1024]{2,1,0:T(8,128)S(1)} %get-tuple-element.7.ga, f32[8,2,16,128]{3,2,1,0:T(8,128)S(1)} %get-tuple-element.8.gb), custom_call_target="tpu_custom_call" | custom-call | tf_op jit(solution)/shard_map/store_outputs/pallas_call | solution.py:478
